TPU v7x, 32 devices: a whole 2x2x4 slice. The times are simulated.
32 devices in a mesh: frame: 4 (over y, core), row: 4 (over z), col: 2 (over x).
Axes of the slice: x: 2, y: 2, z: 4, core: 2. Of those that a mesh axis runs over, the one named last changes fastest.
Arguments:
- queries: bfloat16 [4, 4, 2, 384, 256], P('frame', 'row', 'col'), may hold values from -8 to 8
- key_vectors: bfloat16 [4, 4, 2, 384, 256], P('frame', 'row', 'col'), may hold values from -8 to 8
- value_vectors: bfloat16 [4, 4, 2, 384, 256], P('frame', 'row', 'col'), may hold values from -6 to 6
- forward_out: bfloat16 [4, 4, 2, 384, 256], P('frame', 'row', 'col'), may hold values from -6 to 6
- cotangent: bfloat16 [4, 4, 2, 384, 256], P('frame', 'row', 'col'), may hold values from -48 to 48
- log_norm: float32 [4, 4, 2, 2, 384], P('frame', 'row', 'col'), may hold values from 5 to 14
Outputs:
- grad_queries: bfloat16 [4, 4, 2, 384, 256], P('frame', 'row', 'col')
- grad_keys: bfloat16 [4, 4, 2, 384, 256], P('frame', 'row', 'col')
- grad_values: bfloat16 [4, 4, 2, 384, 256], P('frame', 'row', 'col')
All inputs are finite; a program needn't handle non-finite values.
Results may differ from a plain program's by a relative error of at most 0.006.
Values may be sent and summed in bfloat16 or wider, within the bound.
A program may use at most 128 MiB of HBM per device.

v0:
```python
import jax
import jax.numpy as jnp
from jax import lax
from jax.sharding import PartitionSpec as P


def passed_along(x, axis, by):
    peers = lax.axis_size(axis)
    pairs = [(i, i + by) for i in range(peers) if 0 <= i + by < peers]
    return lax.ppermute(x, axis, pairs)


def with_halo(x, sides, width):
    for axis, dim in sides:
        peers, length = (lax.axis_size(axis), x.shape[dim])
        up = [(i, (i + 1) % peers) for i in range(peers - 1)]
        down = [(j, i) for i, j in up]
        last = lax.slice_in_dim(x, length - width, length, axis=dim)
        leading = lax.slice_in_dim(x, 0, width, axis=dim)
        before = lax.ppermute(last, axis, up)
        after = lax.ppermute(leading, axis, down)
        x = jnp.concatenate([before, x, after], axis=dim)
    return x


def window_valid():
    offsets = jnp.arange(3, dtype=jnp.int32) - 1
    frame_pos = lax.axis_index("frame") + offsets
    row_pos = lax.axis_index("row") + offsets
    col_pos = lax.axis_index("col") + offsets
    along_f = (frame_pos >= 0) & (frame_pos < lax.axis_size("frame"))
    along_r = (row_pos >= 0) & (row_pos < lax.axis_size("row"))
    along_c = (col_pos >= 0) & (col_pos < lax.axis_size("col"))
    return along_f[:, None, None] & along_r[None, :, None] & along_c[None, None, :]


def reduce_frame(partial_sums, dim):
    from_next = passed_along(lax.index_in_dim(partial_sums, 0, dim, keepdims=False), "frame", -1)
    from_prev = passed_along(lax.index_in_dim(partial_sums, 2, dim, keepdims=False), "frame", 1)
    return lax.index_in_dim(partial_sums, 1, dim, keepdims=False) + from_next + from_prev


def reduce_row(partial_sums, dim):
    from_next = passed_along(lax.index_in_dim(partial_sums, 0, dim, keepdims=False), "row", -1)
    from_prev = passed_along(lax.index_in_dim(partial_sums, 2, dim, keepdims=False), "row", 1)
    return lax.index_in_dim(partial_sums, 1, dim, keepdims=False) + from_next + from_prev


def reduce_col(partial_sums, dim):
    from_next = passed_along(lax.index_in_dim(partial_sums, 0, dim, keepdims=False), "col", -1)
    from_prev = passed_along(lax.index_in_dim(partial_sums, 2, dim, keepdims=False), "col", 1)
    return lax.index_in_dim(partial_sums, 1, dim, keepdims=False) + from_next + from_prev


def fold_back(partial_sums):
    partial_sums = reduce_frame(partial_sums, 0)
    partial_sums = reduce_row(partial_sums, 0)
    return reduce_col(partial_sums, 0)


def local(queries, key_vectors, value_vectors, forward_out, cotangent, log_norm):
    tile_rows = queries.shape[3]
    width = queries.shape[4]
    head_count = log_norm.shape[3]
    head_width = width // head_count
    score_scale = head_width ** (-0.5)
    valid = window_valid().reshape(9, 3)
    own_q = queries.reshape(tile_rows, head_count, head_width)
    own_do = cotangent.reshape(tile_rows, head_count, head_width)
    products = cotangent.astype(jnp.float32) * forward_out.astype(jnp.float32)
    row_delta = jnp.sum(products.reshape(tile_rows, head_count, head_width), axis=-1).T
    own_log = log_norm.reshape(head_count, tile_rows)
    out_shape = (1, 1, 1, tile_rows, width)
    joined = jnp.concatenate((key_vectors, value_vectors), axis=3)
    nearby = with_halo(joined, (("frame", 0), ("row", 1), ("col", 2)), 1)
    nearby = nearby.reshape(9, 3, 2 * tile_rows, width)

    def slab_step(grad_q, inputs):
        slab, valid_slab = inputs
        near_k = slab[:, :tile_rows].reshape(3 * tile_rows, head_count, head_width)
        near_v = slab[:, tile_rows:].reshape(3 * tile_rows, head_count, head_width)
        keep = jnp.repeat(valid_slab, tile_rows)
        scores = (
            jnp.einsum("qhd,khd->hqk", own_q, near_k, preferred_element_type=jnp.float32)
            * score_scale
        )
        probs = jnp.where(keep[None, None, :], jnp.exp(scores - own_log[:, :, None]), 0.0)
        dprobs = jnp.einsum("qhd,khd->hqk", own_do, near_v, preferred_element_type=jnp.float32)
        dscores = (probs * (dprobs - row_delta[:, :, None])).astype(jnp.bfloat16)
        grad_q = grad_q + jnp.einsum(
            "hqk,khd->qhd", dscores, near_k, preferred_element_type=jnp.float32
        )
        grad_k = jnp.einsum("hqk,qhd->khd", dscores, own_q, preferred_element_type=jnp.float32)
        grad_v = jnp.einsum(
            "hqk,qhd->khd", probs.astype(jnp.bfloat16), own_do, preferred_element_type=jnp.float32
        )
        stacked = jnp.concatenate(
            (grad_k.reshape(3, tile_rows, width), grad_v.reshape(3, tile_rows, width)), axis=1
        )
        return (grad_q, stacked)

    zeros = jnp.zeros((tile_rows, head_count, head_width), jnp.float32)
    grad_q, partial_sums = lax.scan(slab_step, zeros, (nearby, valid))
    folded = fold_back(partial_sums.reshape(3, 3, 3, 2 * tile_rows, width))
    grad_queries = grad_q.reshape(tile_rows, width) * score_scale
    grad_keys = folded[:tile_rows] * score_scale
    grad_values = folded[tile_rows:]
    return (
        grad_queries.astype(jnp.bfloat16).reshape(out_shape),
        grad_keys.astype(jnp.bfloat16).reshape(out_shape),
        grad_values.astype(jnp.bfloat16).reshape(out_shape),
    )


def solution(mesh):
    placed = (
        P("frame", "row", "col", None, None),
        P("frame", "row", "col", None, None),
        P("frame", "row", "col", None, None),
        P("frame", "row", "col", None, None),
        P("frame", "row", "col", None, None),
        P("frame", "row", "col", None, None),
    )
    return jax.shard_map(
        local,
        mesh=mesh,
        in_specs=placed,
        out_specs=(
            P("frame", "row", "col", None, None),
            P("frame", "row", "col", None, None),
            P("frame", "row", "col", None, None),
        ),
        check_vma=False,
    )
```

profile of v0, /device:TPU:17, one launch (start us, length us, event | category | flops | bytes accessed | tf_op | source)
XLA Modules:
  0.0 517.2 jit_solution(13403199386309435389)
XLA Ops:
  18.4 20.7 %collective-permute-done.3 = bf16[3,1,1,768,256]{4,3,2,1,0:T(8,128)(2,1)S(1)} collective-permute-done((bf16[3,1,1,768,256]{4,3,2,1,0:T(8,128)(2,1)S(1)}, bf16[3,1,1,768,256]{4,3,2,1,0:T(8,128)(2,1)S(1)}, u32[]{:S(2)}, u32[]{:S(2)}) %collective-permute-start.3) | collective-permute-done | bytes 1179680 | tf_op jit(solution)/shard_map/ppermute | solution.py:21
  44.7 7.6 %collective-permute-start.4 = (bf16[3,3,1,768,256]{4,3,2,1,0:T(8,128)(2,1)}, bf16[3,3,1,768,256]{4,3,2,1,0:T(8,128)(2,1)}, u32[]{:S(2)}, u32[]{:S(2)}) collective-permute-start(bf16[3,3,1,768,256]{4,3,2,1,0:T(8,128)(2,1)} %pad_maximum_fusion.1), channel_id=1, source_target_pairs={{0,1},{2,3},{4,5},{6,7},{8,9},{10,11},{12,13},{14,15},{16,17},{18,... | collective-permute-start | bytes 10616840 | tf_op jit(solution)/shard_map/ppermute | solution.py:20
  66.6 55.1 %collective-permute-done.5 = bf16[3,3,1,768,256]{4,3,2,1,0:T(8,128)(2,1)} collective-permute-done((bf16[3,3,1,768,256]{4,3,2,1,0:T(8,128)(2,1)}, bf16[3,3,1,768,256]{4,3,2,1,0:T(8,128)(2,1)}, u32[]{:S(2)}, u32[]{:S(2)}) %collective-permute-start.5) | collective-permute-done | bytes 3538976 | tf_op jit(solution)/shard_map/ppermute | solution.py:21
  125.2 8.2 %pad_maximum_fusion = bf16[3,3,3,768,256]{4,3,2,1,0:T(8,128)(2,1)} fusion(bf16[3,3,1,768,256]{4,3,2,1,0:T(8,128)(2,1)} %collective-permute-done.5, bf16[3,1,1,768,256]{4,3,2,1,0:T(8,128)(2,1)S(1)} %collective-permute-done.3, bf16[1,1,1,768,256]{4,3,2,1,0:T(8,128)(2,1)S(1)} %collective-permute-done.1, ...), kind=kLoop, calls=%fused_computation.17 | loop fusion | flops 31850496 | bytes 21233664 | tf_op jit(solution)/shard_map/concatenate | solution.py:22
  133.4 224.0 %while.13 = (s32[]{:T(128)}, f32[384,2,128]{0,2,1:T(8,128)}, f32[9,3,768,256]{3,2,1,0:T(8,128)}, bf16[9,3,768,256]{3,2,1,0:T(8,128)(2,1)}, pred[9,3]{1,0:T(8,128...) while((s32[]{:T(128)}, f32[384,2,128]{0,2,1:T(8,128)}, ...), condition=%wide.region_2.3_spmd.clone, body=%wide.region_1.2_spmd.clone.sunk | while | flops 1139441664 | bytes 44051088 | solution.py:103
  150.1 4.8 copy.41
  169.8 4.3 copy.42
  175.1 4.8 copy.41
  200.1 4.8 copy.41
  219.9 4.3 copy.42
  225.1 4.8 copy.41
  244.9 4.3 copy.42
  250.2 4.8 copy.41
  269.9 4.3 copy.42
  275.1 4.8 copy.41
  300.2 4.8 copy.41
  325.2 4.8 copy.41
  350.2 4.8 copy.41
  357.4 11.2 %fusion.17 = (f32[3,3,768,256]{3,2,1,0:T(8,128)}, f32[3,3,768,256]{3,2,1,0:T(8,128)}) fusion(f32[9,3,768,256]{3,2,1,0:T(8,128)} %get-tuple-element.52), kind=kLoop, calls=%fused_computation.46 | loop fusion | bytes 28311552 | tf_op jit(solution)/shard_map/slice | solution.py:38
  374.4 75.2 %collective-permute-done.6 = f32[3,3,768,256]{3,2,1,0:T(8,128)} collective-permute-done((f32[3,3,768,256]{3,2,1,0:T(8,128)}, f32[3,3,768,256]{3,2,1,0:T(8,128)}, u32[]{:S(2)}, u32[]{:S(2)}) %collective-permute-start.6) | collective-permute-done | bytes 7077920 | tf_op jit(solution)/shard_map/ppermute | solution.py:10
  450.8 11.3 %add_add_fusion = f32[3,3,768,256]{3,2,1,0:T(8,128)} fusion(f32[3,3,768,256]{3,2,1,0:T(8,128)} %collective-permute-done.7, f32[3,3,768,256]{3,2,1,0:T(8,128)} %collective-permute-done.6, f32[9,3,768,256]{3,2,1,0:T(8,128)} %get-tuple-element.52), kind=kLoop, calls=%fused_computation.18 | loop fusion | flops 3538944 | bytes 28311552 | tf_op jit(solution)/shard_map/add | solution.py:40
  470.5 24.1 %collective-permute-done.8 = f32[3,768,256]{2,1,0:T(8,128)S(1)} collective-permute-done((f32[3,768,256]{2,1,0:T(8,128)S(1)}, f32[3,768,256]{2,1,0:T(8,128)S(1)}, u32[]{:S(2)}, u32[]{:S(2)}) %collective-permute-start.8) | collective-permute-done | bytes 2359328 | tf_op jit(solution)/shard_map/ppermute | solution.py:10
  501.3 4.9 collective-permute-start.11
  508.0 4.9 collective-permute-done.10
  (199 shorter events, 232.5 us)
Async XLA Ops:
  2.5 9.2 %collective-permute-start.1 = (bf16[1,1,1,768,256]{4,3,2,1,0:T(8,128)(2,1)S(1)}, bf16[1,1,1,768,256]{4,3,2,1,0:T(8,128)(2,1)S(1)}, u32[]{:S(2)}, u32[]{:S(2)}) collective-permute-start(bf16[1,1,1,768,256]{4,3,2,1,0:T(8,128)(2,1)S(1)} %constant_dynamic-update-slice_fusion), channel_id=1, source_target_pairs={{8,0},{16,8},{24,16},{9,1},{17,9},{25,17},{10,2},{18,10},{26,18},{... | collective-permute-start | bytes 1179656 | tf_op jit(solution)/shard_map/ppermute | solution.py:21
  5.1 7.8 %collective-permute-start = (bf16[1,1,1,768,256]{4,3,2,1,0:T(8,128)(2,1)S(1)}, bf16[1,1,1,768,256]{4,3,2,1,0:T(8,128)(2,1)S(1)}, u32[]{:S(2)}, u32[]{:S(2)}) collective-permute-start(bf16[1,1,1,768,256]{4,3,2,1,0:T(8,128)(2,1)S(1)} %constant_dynamic-update-slice_fusion), channel_id=1, source_target_pairs={{0,8},{8,16},{16,24},{1,9},{9,17},{17,25},{2,10},{10,18},{18,26},{... | collective-permute-start | bytes 1179656 | tf_op jit(solution)/shard_map/ppermute | solution.py:20
  13.0 26.0 %collective-permute-start.3 = (bf16[3,1,1,768,256]{4,3,2,1,0:T(8,128)(2,1)S(1)}, bf16[3,1,1,768,256]{4,3,2,1,0:T(8,128)(2,1)S(1)}, u32[]{:S(2)}, u32[]{:S(2)}) collective-permute-start(bf16[3,1,1,768,256]{4,3,2,1,0:T(8,128)(2,1)S(1)} %pad_maximum_fusion.2), channel_id=1, source_target_pairs={{2,0},{4,2},{6,4},{3,1},{5,3},{7,5},{10,8},{12,10},{14,12},{11,9},... | collective-permute-start | bytes 3538952 | tf_op jit(solution)/shard_map/ppermute | solution.py:21
  15.1 26.3 %collective-permute-start.2 = (bf16[3,1,1,768,256]{4,3,2,1,0:T(8,128)(2,1)S(1)}, bf16[3,1,1,768,256]{4,3,2,1,0:T(8,128)(2,1)S(1)}, u32[]{:S(2)}, u32[]{:S(2)}) collective-permute-start(bf16[3,1,1,768,256]{4,3,2,1,0:T(8,128)(2,1)S(1)} %pad_maximum_fusion.2), channel_id=1, source_target_pairs={{0,2},{2,4},{4,6},{1,3},{3,5},{5,7},{8,10},{10,12},{12,14},{9,11},... | collective-permute-start | bytes 3538952 | tf_op jit(solution)/shard_map/ppermute | solution.py:20
  43.4 78.3 %collective-permute-start.5 = (bf16[3,3,1,768,256]{4,3,2,1,0:T(8,128)(2,1)}, bf16[3,3,1,768,256]{4,3,2,1,0:T(8,128)(2,1)}, u32[]{:S(2)}, u32[]{:S(2)}) collective-permute-start(bf16[3,3,1,768,256]{4,3,2,1,0:T(8,128)(2,1)} %pad_maximum_fusion.1), channel_id=1, source_target_pairs={{1,0},{3,2},{5,4},{7,6},{9,8},{11,10},{13,12},{15,14},{17,16},{19,... | collective-permute-start | bytes 10616840 | tf_op jit(solution)/shard_map/ppermute | solution.py:21
  44.7 80.5 %collective-permute-start.4 = (bf16[3,3,1,768,256]{4,3,2,1,0:T(8,128)(2,1)}, bf16[3,3,1,768,256]{4,3,2,1,0:T(8,128)(2,1)}, u32[]{:S(2)}, u32[]{:S(2)}) collective-permute-start(bf16[3,3,1,768,256]{4,3,2,1,0:T(8,128)(2,1)} %pad_maximum_fusion.1), channel_id=1, source_target_pairs={{0,1},{2,3},{4,5},{6,7},{8,9},{10,11},{12,13},{14,15},{16,17},{18,... | collective-permute-start | bytes 10616840 | tf_op jit(solution)/shard_map/ppermute | solution.py:20
  66.6 66.8 %copy-start = (f32[1,1,1,2,384]{4,3,2,1,0:T(2,128)S(1)}, f32[1,1,1,2,384]{4,3,2,1,0:T(2,128)}, u32[]{:S(2)}) copy-start(f32[1,1,1,2,384]{4,3,2,1,0:T(2,128)} %param.13) | copy-start | bytes 9220
  368.6 81.0 %collective-permute-start.6 = (f32[3,3,768,256]{3,2,1,0:T(8,128)}, f32[3,3,768,256]{3,2,1,0:T(8,128)}, u32[]{:S(2)}, u32[]{:S(2)}) collective-permute-start(f32[3,3,768,256]{3,2,1,0:T(8,128)} %get-tuple-element.121), channel_id=1, source_target_pairs={{8,0},{16,8},{24,16},{9,1},{17,9},{25,17},{10,2},{18,10},{26,18},{... | collective-permute-start | bytes 21233672 | tf_op jit(solution)/shard_map/ppermute | solution.py:10
  370.5 80.3 %collective-permute-start.7 = (f32[3,3,768,256]{3,2,1,0:T(8,128)}, f32[3,3,768,256]{3,2,1,0:T(8,128)}, u32[]{:S(2)}, u32[]{:S(2)}) collective-permute-start(f32[3,3,768,256]{3,2,1,0:T(8,128)} %get-tuple-element.122), channel_id=1, source_target_pairs={{0,8},{8,16},{16,24},{1,9},{9,17},{17,25},{2,10},{10,18},{18,26},{... | collective-permute-start | bytes 21233672 | tf_op jit(solution)/shard_map/ppermute | solution.py:10
  465.1 29.6 %collective-permute-start.8 = (f32[3,768,256]{2,1,0:T(8,128)S(1)}, f32[3,768,256]{2,1,0:T(8,128)S(1)}, u32[]{:S(2)}, u32[]{:S(2)}) collective-permute-start(f32[3,768,256]{2,1,0:T(8,128)S(1)} %get-tuple-element.123), channel_id=1, source_target_pairs={{2,0},{4,2},{6,4},{3,1},{5,3},{7,5},{10,8},{12,10},{14,12},{11,9},... | collective-permute-start | bytes 7077896 | tf_op jit(solution)/shard_map/ppermute | solution.py:10
  467.0 29.6 %collective-permute-start.9 = (f32[3,768,256]{2,1,0:T(8,128)S(1)}, f32[3,768,256]{2,1,0:T(8,128)S(1)}, u32[]{:S(2)}, u32[]{:S(2)}) collective-permute-start(f32[3,768,256]{2,1,0:T(8,128)S(1)} %get-tuple-element.124), channel_id=1, source_target_pairs={{0,2},{2,4},{4,6},{1,3},{3,5},{5,7},{8,10},{10,12},{12,14},{9,11},... | collective-permute-start | bytes 7077896 | tf_op jit(solution)/shard_map/ppermute | solution.py:10
  500.0 12.9 %collective-permute-start.10 = (f32[768,256]{1,0:T(8,128)}, f32[768,256]{1,0:T(8,128)S(1)}, u32[]{:S(2)}, u32[]{:S(2)}) collective-permute-start(f32[768,256]{1,0:T(8,128)} %get-tuple-element.125), channel_id=1, source_target_pairs={{1,0},{3,2},{5,4},{7,6},{9,8},{11,10},{13,12},{15,14},{17,16},{19,... | collective-permute-start | bytes 2359304 | tf_op jit(solution)/shard_map/ppermute | solution.py:10
  501.3 13.3 %collective-permute-start.11 = (f32[768,256]{1,0:T(8,128)}, f32[768,256]{1,0:T(8,128)}, u32[]{:S(2)}, u32[]{:S(2)}) collective-permute-start(f32[768,256]{1,0:T(8,128)} %get-tuple-element.126), channel_id=1, source_target_pairs={{0,1},{2,3},{4,5},{6,7},{8,9},{10,11},{12,13},{14,15},{16,17},{18,... | collective-permute-start | bytes 2359304 | tf_op jit(solution)/shard_map/ppermute | solution.py:10
where the time goes:
time: 524 us; the launch traced here: 517 us
  waiting for transfers between devices  195 us (37%)
  local copies, waits for them, and re-layouts  149 us (28%)
  matrix products  88.5 us (17%)
  other arithmetic  45.1 us (9%)
  starting transfers between devices  37.2 us (7%)
    ppermute x6, waiting for transfers between devices, passed_along(): return lax.ppermute(x, axis, pairs)  109 us
    ppermute x3, waiting for transfers between devices, with_halo(): after = lax.ppermute(leading, axis, down)  79.3 us
    transpose x9, local copies, waits for them, and re-layouts, slab_step(): jnp.einsum('hqk,qhd->khd', probs.astype(jnp.bfloat16), own_do, preferred_...  42.8 us
    transpose x9, local copies, waits for them, and re-layouts, slab_step(): jnp.einsum('hqk,qhd->khd', dscores, own_q, preferred_element_type=jnp.flo...  38.7 us
    dot_general x9, matrix products, slab_step(): jnp.einsum('hqk,qhd->khd', probs.astype(jnp.bfloat16), own_do, preferred_...  23.3 us
    dot_general x9, matrix products, slab_step(): jnp.einsum('hqk,khd->qhd', dscores, near_k, preferred_element_type=jnp.fl...  19.4 us
    dot_general x9, matrix products, slab_step(): jnp.einsum('qhd,khd->hqk', own_q, near_k, preferred_element_type=jnp.floa...  17.7 us
    ppermute x6, starting transfers between devices, passed_along(): return lax.ppermute(x, axis, pairs)  17.4 us
  transfers between devices with their start and end apart: 12, of which 12 were waited for; matrix products, arithmetic and copies ran while one was open for 3% of the time, Pallas kernels for 0%

commit v1 on v0

--- a/solution.py
+++ b/solution.py
@@ -1,7 +1,14 @@
+import functools
+
 import jax
 import jax.numpy as jnp
 from jax import lax
+from jax.experimental import pallas as pl
+from jax.experimental.pallas import tpu as pltpu
 from jax.sharding import PartitionSpec as P
+
+MESH = pl.DeviceIdType.MESH
+LOG2E = 1.4426950408889634
 
 
 def passed_along(x, axis, by):
@@ -112,23 +119,338 @@
     )
 
 
+def arrived(ref, sem):
+    pltpu.make_async_copy(ref, ref, sem).wait()
+
+
+def window_kernel(
+    rows,
+    q_ref, k_ref, v_ref, o_ref, do_ref, log_ref,
+    dq_ref, dk_ref, dv_ref,
+    kv, qd, stat, stat_own, grads_out, grads_in, own_sum, partial, dq_sum, dq_in, final_kv, final_q,
+    kv_send, kv_recv, q_send, q_recv, pass_send, halo_send, halo_recv,
+    ret_send, ret_recv, dq_send, dq_recv, out_send, out_recv,
+):
+    f, r, b = lax.axis_index("frame"), lax.axis_index("row"), lax.axis_index("col")
+    y, a = f // 2, f % 2
+    tokens, width = q_ref.shape
+    feats = width // 2
+    scale = feats ** (-0.5)
+    other_f = 2 * y + 1 - a
+    across_f = f + 2 - 4 * y
+    near = 1 - y
+    has_row = {-1: r > 0, 1: r < rows - 1}
+
+    barrier = pltpu.get_barrier_semaphore()
+
+    def greet(where):
+        pl.semaphore_signal(barrier, inc=1, device_id=where, device_id_type=MESH)
+
+    for where in ((other_f, r, b), (f, r, 1 - b), (other_f, r, 1 - b), (across_f, r, b)):
+        greet(where)
+    for step in (-1, 1):
+        @pl.when(has_row[step])
+        def _():
+            greet((f, r + step, b))
+            greet((across_f, r + step, b))
+
+    def cols(head):
+        return pl.ds(pl.multiple_of(head * feats, feats), feats)
+
+    def toks(col):
+        return pl.ds(pl.multiple_of(col * tokens, 128), tokens)
+
+    ones = jnp.ones((8, feats), jnp.bfloat16)
+    along = (((1,), (1,)), ((), ()))
+    for head in range(2):
+        part = slice(head * feats, (head + 1) * feats)
+        product = do_ref[:, part].astype(jnp.float32) * o_ref[:, part].astype(jnp.float32)
+        high = product.astype(jnp.bfloat16)
+        low = (product - high.astype(jnp.float32)).astype(jnp.bfloat16)
+        delta = lax.dot_general(ones, high, along, preferred_element_type=jnp.float32)
+        delta += lax.dot_general(ones, low, along, preferred_element_type=jnp.float32)
+        stat_own[head] = delta
+        stat_own[head, 0:1, :] = log_ref[head : head + 1, :] * LOG2E
+    dq_sum[...] = jnp.zeros_like(dq_sum)
+
+    pl.semaphore_wait(
+        barrier, 4 + 2 * (has_row[-1].astype(jnp.int32) + has_row[1].astype(jnp.int32))
+    )
+
+    def remote(src, dst, send, recv, where):
+        return pltpu.make_async_remote_copy(
+            src_ref=src, dst_ref=dst, send_sem=send, recv_sem=recv, device_id=where, device_id_type=MESH
+        )
+
+    key_f = 2 * y + b
+    stays = a == b
+    for kind, ref in enumerate((k_ref, v_ref)):
+        remote(
+            ref.at[:, cols(1 - b)], kv.at[1, a, kind], kv_send.at[0, kind], kv_recv.at[a, kind],
+            (key_f, r, 1 - b),
+        ).start()
+    for kind, ref in enumerate((k_ref, v_ref)):
+        src, dst = ref.at[:, cols(b)], kv.at[1, a, kind]
+
+        @pl.when(stays)
+        def _():
+            pltpu.make_async_copy(src, dst, kv_recv.at[a, kind]).start()
+
+        @pl.when(jnp.logical_not(stays))
+        def _():
+            remote(src, dst, kv_send.at[1, kind], kv_recv.at[a, kind], (key_f, r, b)).start()
+
+    def q_slot(kind, frame, col):
+        if kind == 2:
+            return stat.at[frame, :, toks(col)]
+        return qd.at[frame, kind, toks(col)]
+
+    def q_source(kind, head):
+        if kind == 2:
+            return stat_own.at[head]
+        return (q_ref, do_ref)[kind].at[:, cols(head)]
+
+    for kind in range(3):
+        remote(
+            q_source(kind, 1 - b), q_slot(kind, a, b), q_send.at[0, kind], q_recv.at[a, b, kind],
+            (f, r, 1 - b),
+        ).start()
+    for kind in range(3):
+        remote(
+            q_source(kind, b), q_slot(kind, a, b), q_send.at[1, kind], q_recv.at[a, b, kind],
+            (other_f, r, b),
+        ).start()
+        pltpu.make_async_copy(q_source(kind, b), q_slot(kind, a, b), q_recv.at[a, b, kind]).start()
+
+    for frame in range(2):
+        for kind in range(2):
+            arrived(kv.at[1, frame, kind], kv_recv.at[frame, kind])
+        for step in (-1, 1):
+            @pl.when(has_row[step])
+            def _():
+                remote(
+                    kv.at[1, frame], kv.at[1 - step, frame], halo_send.at[1 - step, frame],
+                    halo_recv.at[1 - step, frame], (f, r + step, b),
+                ).start()
+
+        @pl.when(near == frame)
+        def _():
+            remote(
+                kv.at[1, frame], kv.at[1, 2], halo_send.at[1, 2], halo_recv.at[1, 2], (across_f, r, b)
+            ).start()
+            for step in (-1, 1):
+                @pl.when(has_row[step])
+                def _():
+                    remote(
+                        kv.at[1, frame], kv.at[1 - step, 2], halo_send.at[1 - step, 2],
+                        halo_recv.at[1 - step, 2], (across_f, r + step, b),
+                    ).start()
+
+    for kind in range(3):
+        arrived(q_slot(kind, a, 1 - b), q_recv.at[a, 1 - b, kind])
+        remote(
+            q_slot(kind, a, 1 - b), q_slot(kind, a, 1 - b), pass_send.at[kind],
+            q_recv.at[a, 1 - b, kind], (other_f, r, b),
+        ).start()
+    for frame, col in ((a, b), (1 - a, b), (1 - a, 1 - b)):
+        for kind in range(3):
+            arrived(q_slot(kind, frame, col), q_recv.at[frame, col, kind])
+
+    chunk = 256
+    count = 2 * tokens // chunk
+
+    def one_frame(at_row, at_frame, frame):
+        keys = kv[at_row, at_frame, 0]
+        values = kv[at_row, at_frame, 1]
+
+        def products(at):
+            some = slice(at * chunk, (at + 1) * chunk)
+            q_part = qd[frame, 0, some, :]
+            do_part = qd[frame, 1, some, :]
+            scores = lax.dot_general(keys, q_part, along, preferred_element_type=jnp.float32)
+            dprobs = lax.dot_general(values, do_part, along, preferred_element_type=jnp.float32)
+            return q_part, do_part, scores, dprobs
+
+        dk = dv = None
+        upcoming = products(0)
+        for at in range(count):
+            some = slice(at * chunk, (at + 1) * chunk)
+            q_part, do_part, scores, dprobs = upcoming
+            if at + 1 < count:
+                upcoming = products(at + 1)
+            probs = jnp.exp2(scores * (scale * LOG2E) - stat[frame, 0:1, some])
+            dscores = probs * (dprobs - stat[frame, 1:2, some])
+            probs = probs.astype(jnp.bfloat16)
+            dscores = dscores.astype(jnp.bfloat16)
+            dv_part = jnp.dot(probs, do_part, preferred_element_type=jnp.float32)
+            dk_part = jnp.dot(dscores, q_part, preferred_element_type=jnp.float32)
+            dv = dv_part if dv is None else dv + dv_part
+            dk = dk_part if dk is None else dk + dk_part
+            dq_sum[frame, some, :] += lax.dot_general(
+                dscores, keys, (((0,), (0,)), ((), ())), preferred_element_type=jnp.float32
+            )
+        partial[0] += dk
+        partial[1] += dv
+
+    def one_tile(at, carry):
+        at_row, at_frame = (at // 3 + 1) % 3, at % 3
+        to_row = r + at_row - 1
+        outer = at_frame // 2
+
+        @pl.when((to_row >= 0) & (to_row < rows))
+        def _():
+            @pl.when(at >= 2)
+            def _():
+                arrived(kv.at[at_row, at_frame], halo_recv.at[at_row, at_frame])
+
+            partial[...] = jnp.zeros_like(partial)
+
+            def over_frames(step, carry):
+                one_frame(at_row, at_frame, step + near * outer)
+                return carry
+
+            lax.fori_loop(0, 2 - outer, over_frames, 0)
+
+            @pl.when(at < 2)
+            def _():
+                own_sum[at_frame] = partial[...]
+
+            @pl.when(at >= 2)
+            def _():
+                grads_out[at_row, at_frame] = partial[...].astype(jnp.bfloat16)
+                remote(
+                    grads_out.at[at_row, at_frame], grads_in.at[2 - at_row, at_frame],
+                    ret_send.at[at_row, at_frame], ret_recv.at[2 - at_row, at_frame],
+                    (f + outer * (2 - 4 * y), to_row, b),
+                ).start()
+
+        return carry
+
+    lax.fori_loop(0, 9, one_tile, 0)
+
+    dq_copy = remote(dq_sum.at[1 - a], dq_in, dq_send, dq_recv, (other_f, r, b))
+    dq_copy.start()
+    dq_copy.wait_recv()
+    final_q[...] = ((dq_sum[a] + dq_in[...]) * scale).astype(jnp.bfloat16)
+    mine = pltpu.make_async_copy(final_q.at[toks(b)], dq_ref.at[:, cols(b)], out_recv.at[0, b])
+    mine.start()
+    remote(
+        final_q.at[toks(1 - b)], dq_ref.at[:, cols(b)], out_send.at[2, 0], out_recv.at[0, b], (f, r, 1 - b)
+    ).start()
+
+    for frame in range(2):
+        for step in (-1, 1):
+            @pl.when(has_row[step])
+            def _():
+                arrived(grads_in.at[1 + step, frame], ret_recv.at[1 + step, frame])
+                own_sum[frame] += grads_in[1 + step, frame].astype(jnp.float32)
+
+        @pl.when(near == frame)
+        def _():
+            arrived(grads_in.at[1, 2], ret_recv.at[1, 2])
+            own_sum[frame] += grads_in[1, 2].astype(jnp.float32)
+            for step in (-1, 1):
+                @pl.when(has_row[step])
+                def _():
+                    arrived(grads_in.at[1 + step, 2], ret_recv.at[1 + step, 2])
+                    own_sum[frame] += grads_in[1 + step, 2].astype(jnp.float32)
+
+        final_kv[frame, 0] = (own_sum[frame, 0] * scale).astype(jnp.bfloat16)
+        final_kv[frame, 1] = own_sum[frame, 1].astype(jnp.bfloat16)
+        stays_here = (a == frame) & (a == b)
+        for kind, ref in enumerate((dk_ref, dv_ref)):
+            src, dst = final_kv.at[frame, kind], ref.at[:, cols(b)]
+
+            @pl.when(stays_here)
+            def _():
+                pltpu.make_async_copy(src, dst, out_recv.at[1 + kind, b]).start()
+
+            @pl.when(jnp.logical_not(stays_here))
+            def _():
+                remote(
+                    src, dst, out_send.at[frame, kind], out_recv.at[1 + kind, b], (2 * y + frame, r, a)
+                ).start()
+
+    for kind in range(3):
+        out = (dq_ref, dk_ref, dv_ref)[kind]
+        for head in range(2):
+            arrived(out.at[:, head * feats : (head + 1) * feats], out_recv.at[kind, head])
+    dq_copy.wait_send()
+    arrived(final_q.at[toks(1 - b)], out_send.at[2, 0])
+    for kind in range(2):
+        arrived(kv.at[1, 0, kind], kv_send.at[0, kind])
+
+        @pl.when(jnp.logical_not(stays))
+        def _():
+            arrived(kv.at[1, 0, kind], kv_send.at[1, kind])
+
+        for frame in range(2):
+            @pl.when(jnp.logical_not((a == frame) & (a == b)))
+            def _():
+                arrived(final_kv.at[frame, kind], out_send.at[frame, kind])
+
+    for kind in range(3):
+        for which in range(2):
+            arrived(q_source(kind, 0), q_send.at[which, kind])
+        arrived(q_source(kind, 0), pass_send.at[kind])
+    arrived(kv.at[1, 2], halo_send.at[1, 2])
+    arrived(grads_out.at[1, 2], ret_send.at[1, 2])
+    for step in (-1, 1):
+        @pl.when(has_row[step])
+        def _():
+            for frame in range(3):
+                arrived(kv.at[1 - step, frame], halo_send.at[1 - step, frame])
+                arrived(grads_out.at[1 + step, frame], ret_send.at[1 + step, frame])
+
+
+def local_window(rows, queries, key_vectors, value_vectors, forward_out, cotangent, log_norm):
+    shape = queries.shape
+    tokens, width = shape[3:]
+    feats = width // 2
+    flat = [x.reshape(tokens, width) for x in (queries, key_vectors, value_vectors, forward_out, cotangent)]
+    half = (tokens, feats)
+    low, full = jnp.bfloat16, jnp.float32
+    dma = pltpu.SemaphoreType.DMA
+    any_space = pl.BlockSpec(memory_space=pl.ANY)
+    vmem = pl.BlockSpec(memory_space=pltpu.VMEM)
+    outs = pl.pallas_call(
+        functools.partial(window_kernel, rows),
+        out_shape=[jax.ShapeDtypeStruct((tokens, width), low)] * 3,
+        in_specs=[any_space, any_space, any_space, vmem, vmem, vmem],
+        out_specs=[any_space] * 3,
+        scratch_shapes=[
+            pltpu.VMEM((3, 3, 2) + half, low),
+            pltpu.VMEM((2, 2, 2 * tokens, feats), low),
+            pltpu.VMEM((2, 8, 2 * tokens), full),
+            pltpu.VMEM((2, 8, tokens), full),
+            pltpu.VMEM((3, 3, 2) + half, low),
+            pltpu.VMEM((3, 3, 2) + half, low),
+            pltpu.VMEM((2, 2) + half, full),
+            pltpu.VMEM((2,) + half, full),
+            pltpu.VMEM((2, 2 * tokens, feats), full),
+            pltpu.VMEM((2 * tokens, feats), full),
+            pltpu.VMEM((2, 2) + half, low),
+            pltpu.VMEM((2 * tokens, feats), low),
+            dma((2, 2)), dma((2, 2)), dma((2, 3)), dma((2, 2, 3)), dma((3,)), dma((3, 3)), dma((3, 3)),
+            dma((3, 3)), dma((3, 3)), dma, dma, dma((3, 2)), dma((3, 2)),
+        ],
+        compiler_params=pltpu.CompilerParams(
+            collective_id=0, has_side_effects=True, vmem_limit_bytes=40 * 2**20
+        ),
+    )(*flat, log_norm.reshape(2, tokens))
+    return tuple(x.reshape(shape) for x in outs)
+
+
 def solution(mesh):
-    placed = (
-        P("frame", "row", "col", None, None),
-        P("frame", "row", "col", None, None),
-        P("frame", "row", "col", None, None),
-        P("frame", "row", "col", None, None),
-        P("frame", "row", "col", None, None),
-        P("frame", "row", "col", None, None),
-    )
+    placed = (P("frame", "row", "col", None, None),) * 6
+    sizes = dict(mesh.shape)
+    body = local
+    if sizes["frame"] == 4 and sizes["col"] == 2:
+        body = functools.partial(local_window, sizes["row"])
     return jax.shard_map(
-        local,
+        body,
         mesh=mesh,
         in_specs=placed,
-        out_specs=(
-            P("frame", "row", "col", None, None),
-            P("frame", "row", "col", None, None),
-            P("frame", "row", "col", None, None),
-        ),
+        out_specs=placed[:3],
         check_vma=False,
     )

time: 524 us -> 56.5 us (0.11)
  the two profiles are of different devices: /device:TPU:17 before, /device:TPU:13 now
where the time goes in v1:
time: 56.5 us; the launch traced here: 56.3 us
  Pallas kernels  48.3 us (85%)
  local copies, waits for them, and re-layouts  7.34 us (13%)
  between operations  0.65 us (1%)
    pallas_call x1, Pallas kernels, local_window(): pl.pallas_call(functools.partial(window_kernel, rows), out_shape=[jax.Sha...  48.3 us
    unnamed x15, local copies, waits for them, and re-layouts  7.34 us

profile of v1, /device:TPU:13, one launch (start us, length us, event | category | flops | bytes accessed | tf_op | source)
XLA Modules:
  0.0 56.3 jit_solution(12186475739801366400)
XLA Ops:
  0.6 0.0 copy-start.5
  0.6 0.7 %copy-done.5 = f32[1,1,1,2,384]{4,3,2,1,0:T(2,128)S(1)} copy-done((f32[1,1,1,2,384]{4,3,2,1,0:T(2,128)S(1)}, f32[1,1,1,2,384]{4,3,2,1,0:T(2,128)}, u32[]{:S(2)}) %copy-start.5) | copy-done | bytes 3096
  1.3 0.0 copy-start
  1.3 0.9 %copy-done = bf16[1,1,1,384,256]{4,3,2,1,0:T(8,128)(2,1)S(1)} copy-done((bf16[1,1,1,384,256]{4,3,2,1,0:T(8,128)(2,1)S(1)}, bf16[1,1,1,384,256]{4,3,2,1,0:T(8,128)(2,1)}, u32[]{:S(2)}) %copy-start) | copy-done | bytes 196632
  2.2 0.0 copy-start.1
  2.2 0.9 %copy-done.1 = bf16[1,1,1,384,256]{4,3,2,1,0:T(8,128)(2,1)S(1)} copy-done((bf16[1,1,1,384,256]{4,3,2,1,0:T(8,128)(2,1)S(1)}, bf16[1,1,1,384,256]{4,3,2,1,0:T(8,128)(2,1)}, u32[]{:S(2)}) %copy-start.1) | copy-done | bytes 196632
  3.2 0.0 copy-start.2
  3.2 0.9 %copy-done.2 = bf16[1,1,1,384,256]{4,3,2,1,0:T(8,128)(2,1)S(1)} copy-done((bf16[1,1,1,384,256]{4,3,2,1,0:T(8,128)(2,1)S(1)}, bf16[1,1,1,384,256]{4,3,2,1,0:T(8,128)(2,1)}, u32[]{:S(2)}) %copy-start.2) | copy-done | bytes 196632
  4.1 0.0 copy-start.3
  4.1 0.9 %copy-done.3 = bf16[1,1,1,384,256]{4,3,2,1,0:T(8,128)(2,1)S(1)} copy-done((bf16[1,1,1,384,256]{4,3,2,1,0:T(8,128)(2,1)S(1)}, bf16[1,1,1,384,256]{4,3,2,1,0:T(8,128)(2,1)}, u32[]{:S(2)}) %copy-start.3) | copy-done | bytes 196632
  5.0 0.0 copy-start.4
  5.0 0.9 %copy-done.4 = bf16[1,1,1,384,256]{4,3,2,1,0:T(8,128)(2,1)S(1)} copy-done((bf16[1,1,1,384,256]{4,3,2,1,0:T(8,128)(2,1)S(1)}, bf16[1,1,1,384,256]{4,3,2,1,0:T(8,128)(2,1)}, u32[]{:S(2)}) %copy-start.4) | copy-done | bytes 196632
  6.0 48.3 %shard_map.85 = (bf16[384,256]{1,0:T(8,128)(2,1)S(1)}, bf16[384,256]{1,0:T(8,128)(2,1)S(1)}, bf16[384,256]{1,0:T(8,128)(2,1)S(1)}) custom-call(bf16[384,256]{1,0:T(8,128)(2,1)S(1)} %bitcast.12, bf16[384,256]{1,0:T(8,128)(2,1)S(1)} %bitcast.13, bf16[384,256]{1,0:T(8,128)(2,1)S(1)} %bitcast.14, bf16[384,256]{1,0:T(8,128)(2,1)S(1)} %bitcast.15, ...), custom_call_target="tpu_custom_call" | custom-call | tf_op jit(solution)/shard_map/pallas_call | solution.py:416
  54.2 0.7 %copy.12 = bf16[1,1,1,384,256]{4,3,2,1,0:T(8,128)(2,1)} copy(bf16[1,1,1,384,256]{4,3,2,1,0:T(8,128)(2,1)S(1)} %bitcast.11) | data formatting | bytes 393216
  54.9 0.7 %copy.13 = bf16[1,1,1,384,256]{4,3,2,1,0:T(8,128)(2,1)} copy(bf16[1,1,1,384,256]{4,3,2,1,0:T(8,128)(2,1)S(1)} %bitcast.10) | data formatting | bytes 393216
  55.6 0.7 %copy.14 = bf16[1,1,1,384,256]{4,3,2,1,0:T(8,128)(2,1)} copy(bf16[1,1,1,384,256]{4,3,2,1,0:T(8,128)(2,1)S(1)} %bitcast.9) | data formatting | bytes 393216
Async XLA Ops:
  0.6 0.7 %copy-start.5 = (f32[1,1,1,2,384]{4,3,2,1,0:T(2,128)S(1)}, f32[1,1,1,2,384]{4,3,2,1,0:T(2,128)}, u32[]{:S(2)}) copy-start(f32[1,1,1,2,384]{4,3,2,1,0:T(2,128)} %param.11) | copy-start | bytes 9220
  1.3 0.9 %copy-start = (bf16[1,1,1,384,256]{4,3,2,1,0:T(8,128)(2,1)S(1)}, bf16[1,1,1,384,256]{4,3,2,1,0:T(8,128)(2,1)}, u32[]{:S(2)}) copy-start(bf16[1,1,1,384,256]{4,3,2,1,0:T(8,128)(2,1)} %param.6) | copy-start | bytes 589828
  2.2 0.9 %copy-start.1 = (bf16[1,1,1,384,256]{4,3,2,1,0:T(8,128)(2,1)S(1)}, bf16[1,1,1,384,256]{4,3,2,1,0:T(8,128)(2,1)}, u32[]{:S(2)}) copy-start(bf16[1,1,1,384,256]{4,3,2,1,0:T(8,128)(2,1)} %param.7) | copy-start | bytes 589828
  3.2 0.9 %copy-start.2 = (bf16[1,1,1,384,256]{4,3,2,1,0:T(8,128)(2,1)S(1)}, bf16[1,1,1,384,256]{4,3,2,1,0:T(8,128)(2,1)}, u32[]{:S(2)}) copy-start(bf16[1,1,1,384,256]{4,3,2,1,0:T(8,128)(2,1)} %param.8) | copy-start | bytes 589828
  4.1 0.9 %copy-start.3 = (bf16[1,1,1,384,256]{4,3,2,1,0:T(8,128)(2,1)S(1)}, bf16[1,1,1,384,256]{4,3,2,1,0:T(8,128)(2,1)}, u32[]{:S(2)}) copy-start(bf16[1,1,1,384,256]{4,3,2,1,0:T(8,128)(2,1)} %param.9) | copy-start | bytes 589828
  5.0 0.9 %copy-start.4 = (bf16[1,1,1,384,256]{4,3,2,1,0:T(8,128)(2,1)S(1)}, bf16[1,1,1,384,256]{4,3,2,1,0:T(8,128)(2,1)}, u32[]{:S(2)}) copy-start(bf16[1,1,1,384,256]{4,3,2,1,0:T(8,128)(2,1)} %param.10) | copy-start | bytes 589828

commit v2 on v0

--- a/solution.py
+++ b/solution.py
@@ -1,7 +1,14 @@
+import functools
+
 import jax
 import jax.numpy as jnp
 from jax import lax
+from jax.experimental import pallas as pl
+from jax.experimental.pallas import tpu as pltpu
 from jax.sharding import PartitionSpec as P
+
+MESH = pl.DeviceIdType.MESH
+LOG2E = 1.4426950408889634
 
 
 def passed_along(x, axis, by):
@@ -112,23 +119,351 @@
     )
 
 
+def arrived(ref, sem):
+    pltpu.make_async_copy(ref, ref, sem).wait()
+
+
+def window_kernel(
+    rows,
+    q_ref, k_ref, v_ref, o_ref, do_ref, log_ref,
+    dq_ref, dk_ref, dv_ref,
+    kv, qd, stat, stat_own, o_in, do_in, log_in, grads_out, grads_in, sums, dq_sum, dq_out, dq_in,
+    final_kv, final_q,
+    load_sem, kv_send, kv_recv, q_send, q_recv, halo_send, halo_recv,
+    ret_send, ret_recv, dq_send, dq_recv, out_send, out_recv,
+):
+    f, r, b = lax.axis_index("frame"), lax.axis_index("row"), lax.axis_index("col")
+    y, a = f // 2, f % 2
+    tokens, width = q_ref.shape
+    feats = width // 2
+    scale = feats ** (-0.5)
+    other_f = 2 * y + 1 - a
+    across_f = f + 2 - 4 * y
+    near = 1 - y
+    has_row = {-1: r > 0, 1: r < rows - 1}
+
+    barrier = pltpu.get_barrier_semaphore()
+
+    def greet(where):
+        pl.semaphore_signal(barrier, inc=1, device_id=where, device_id_type=MESH)
+
+    for where in ((other_f, r, b), (f, r, 1 - b), (other_f, r, 1 - b), (across_f, r, b)):
+        greet(where)
+    for step in (-1, 1):
+        @pl.when(has_row[step])
+        def _():
+            greet((f, r + step, b))
+            greet((across_f, r + step, b))
+
+    def cols(head):
+        return pl.ds(pl.multiple_of(head * feats, feats), feats)
+
+    def toks(frame):
+        return pl.ds(pl.multiple_of(frame * tokens, 128), tokens)
+
+    def remote(src, dst, send, recv, where):
+        return pltpu.make_async_remote_copy(
+            src_ref=src, dst_ref=dst, send_sem=send, recv_sem=recv, device_id=where, device_id_type=MESH
+        )
+
+    def q_slot(kind, frame, col):
+        if kind == 2:
+            return stat.at[col, :, toks(frame)]
+        return qd.at[col, kind, toks(frame)]
+
+    def q_source(kind, head):
+        if kind == 2:
+            return stat_own.at[head]
+        return (q_ref, do_ref)[kind].at[:, cols(head)]
+
+    def q_local(kind):
+        pltpu.make_async_copy(q_source(kind, a), q_slot(kind, a, b), q_recv.at[b, a, kind]).start()
+
+    def q_remote(kind, which):
+        head, col = ((1 - a, b), (a, 1 - b), (1 - a, 1 - b))[which]
+        remote(
+            q_source(kind, head), q_slot(kind, a, b), q_send.at[which, kind], q_recv.at[b, a, kind],
+            (2 * y + head, r, col),
+        ).start()
+
+    loads = [
+        pltpu.make_async_copy(src, dst, load_sem.at[at])
+        for at, (src, dst) in enumerate(((do_ref, do_in), (o_ref, o_in), (log_ref, log_in)))
+    ]
+    for kind, ref in enumerate((k_ref, v_ref)):
+        pltpu.make_async_copy(ref.at[:, cols(a)], kv.at[1, a, kind], kv_recv.at[a, kind]).start()
+    for load in loads:
+        load.start()
+    for kind in range(2):
+        q_local(kind)
+
+    pl.semaphore_wait(
+        barrier, 4 + 2 * (has_row[-1].astype(jnp.int32) + has_row[1].astype(jnp.int32))
+    )
+
+    for kind, ref in enumerate((k_ref, v_ref)):
+        remote(
+            ref.at[:, cols(1 - a)], kv.at[1, a, kind], kv_send.at[kind], kv_recv.at[a, kind], (other_f, r, b)
+        ).start()
+    for which in range(3):
+        for kind in range(2):
+            q_remote(kind, which)
+
+    for frame in (a, 1 - a):
+        for kind in range(2):
+            arrived(kv.at[1, frame, kind], kv_recv.at[frame, kind])
+        for step in (-1, 1):
+            @pl.when(has_row[step])
+            def _():
+                remote(
+                    kv.at[1, frame], kv.at[1 - step, frame], halo_send.at[1 - step, frame],
+                    halo_recv.at[1 - step, frame], (f, r + step, b),
+                ).start()
+
+        @pl.when(near == frame)
+        def _():
+            remote(
+                kv.at[1, frame], kv.at[1, 2], halo_send.at[1, 2], halo_recv.at[1, 2], (across_f, r, b)
+            ).start()
+            for step in (-1, 1):
+                @pl.when(has_row[step])
+                def _():
+                    remote(
+                        kv.at[1, frame], kv.at[1 - step, 2], halo_send.at[1 - step, 2],
+                        halo_recv.at[1 - step, 2], (across_f, r + step, b),
+                    ).start()
+
+    for load in loads:
+        load.wait()
+    ones = jnp.ones((8, feats), jnp.bfloat16)
+    along = (((1,), (1,)), ((), ()))
+    for head in range(2):
+        part = slice(head * feats, (head + 1) * feats)
+        product = do_in[:, part].astype(jnp.float32) * o_in[:, part].astype(jnp.float32)
+        high = product.astype(jnp.bfloat16)
+        low = (product - high.astype(jnp.float32)).astype(jnp.bfloat16)
+        delta = lax.dot_general(ones, high, along, preferred_element_type=jnp.float32)
+        delta += lax.dot_general(ones, low, along, preferred_element_type=jnp.float32)
+        stat_own[head] = delta
+        stat_own[head, 0:1, :] = log_in[head : head + 1, :] * LOG2E
+    q_local(2)
+    for which in range(3):
+        q_remote(2, which)
+    dq_sum[...] = jnp.zeros_like(dq_sum)
+
+    def one_block(at_row, at_frame, col, first):
+        keys = kv[at_row, at_frame, 0]
+        values = kv[at_row, at_frame, 1]
+        keys_t = keys.T
+        if isinstance(at_frame, int) and at_frame == 2:
+            chunks = [toks(near)]
+        else:
+            chunks = [pl.ds(at, 256) for at in range(0, 2 * tokens, 256)]
+
+        def products(some):
+            q_part = qd[col, 0, some, :]
+            do_part = qd[col, 1, some, :]
+            scores = lax.dot_general(keys, q_part, along, preferred_element_type=jnp.float32)
+            dprobs = lax.dot_general(values, do_part, along, preferred_element_type=jnp.float32)
+            return q_part, do_part, scores, dprobs
+
+        dk = dv = None
+        upcoming = products(chunks[0])
+        for at, some in enumerate(chunks):
+            q_part, do_part, scores, dprobs = upcoming
+            if at + 1 < len(chunks):
+                upcoming = products(chunks[at + 1])
+            probs = jnp.exp2(scores * (scale * LOG2E) - stat[col, 0:1, some])
+            dscores = probs * (dprobs - stat[col, 1:2, some])
+            probs = probs.astype(jnp.bfloat16)
+            dscores = dscores.astype(jnp.bfloat16)
+            dv_part = jnp.dot(probs, do_part, preferred_element_type=jnp.float32)
+            dk_part = jnp.dot(dscores, q_part, preferred_element_type=jnp.float32)
+            dv = dv_part if dv is None else dv + dv_part
+            dk = dk_part if dk is None else dk + dk_part
+            dq_sum[col, :, some] += jnp.dot(keys_t, dscores, preferred_element_type=jnp.float32)
+        if first:
+            sums[at_row, at_frame, 0] = dk
+            sums[at_row, at_frame, 1] = dv
+        else:
+            sums[at_row, at_frame, 0] += dk
+            sums[at_row, at_frame, 1] += dv
+
+    def give_back(at_row, at_frame):
+        grads_out[at_row, at_frame] = sums[at_row, at_frame].astype(jnp.bfloat16)
+        remote(
+            grads_out.at[at_row, at_frame], grads_in.at[2 - at_row, at_frame],
+            ret_send.at[at_row, at_frame], ret_recv.at[2 - at_row, at_frame],
+            (across_f if at_frame == 2 else f, r + at_row - 1, b),
+        ).start()
+
+    def q_arrived(col):
+        for frame in range(2):
+            for kind in range(3):
+                arrived(q_slot(kind, frame, col), q_recv.at[col, frame, kind])
+
+    def own_row(col, first):
+        def body(frame, carry):
+            one_block(1, frame, col, first)
+            return carry
+
+        lax.fori_loop(0, 2, body, 0)
+
+    def both_sides(frame, wait, blocks, back):
+        def body(side, carry):
+            at_row = 2 * side
+            to_row = r + at_row - 1
+
+            @pl.when((to_row >= 0) & (to_row < rows))
+            def _():
+                if wait:
+                    arrived(kv.at[at_row, frame], halo_recv.at[at_row, frame])
+                for col, first in blocks:
+                    one_block(at_row, frame, col, first)
+                if back:
+                    give_back(at_row, frame)
+
+            return carry
+
+        lax.fori_loop(0, 2, body, 0)
+
+    def send_dq(frame, which):
+        dq_out[:, toks(frame)] = dq_sum[1 - b, :, toks(frame)].astype(jnp.bfloat16)
+        remote(
+            dq_out.at[:, toks(frame)], dq_in.at[:, toks(frame)], dq_send.at[which], dq_recv.at[which],
+            (f, r, 1 - b),
+        ).start()
+
+    q_arrived(b)
+    own_row(b, True)
+    arrived(kv.at[1, 2], halo_recv.at[1, 2])
+    one_block(1, 2, b, True)
+    both_sides(0, True, ((b, True),), False)
+    q_arrived(1 - b)
+    both_sides(0, False, ((1 - b, False),), True)
+    one_block(1, 2, 1 - b, False)
+    give_back(1, 2)
+    both_sides(1, True, ((b, True), (1 - b, False)), True)
+    own_row(1 - b, False)
+    send_dq(1 - near, 0)
+    both_sides(2, True, ((1 - b, True), (b, False)), True)
+    send_dq(near, 1)
+
+    def add_back(frame, at_row, at_frame):
+        arrived(grads_in.at[at_row, at_frame], ret_recv.at[at_row, at_frame])
+        sums[1, frame] += grads_in[at_row, at_frame].astype(jnp.float32)
+
+    def finish_keys(frame):
+        for step in (-1, 1):
+            @pl.when(has_row[step])
+            def _():
+                add_back(frame, 1 + step, frame)
+
+    def hand_out(kind, frame, src, ref):
+        dst = ref.at[:, cols(a)]
+
+        @pl.when(frame == a)
+        def _():
+            pltpu.make_async_copy(src, dst, out_recv.at[kind, a]).start()
+
+        @pl.when(frame != a)
+        def _():
+            remote(src, dst, out_send.at[kind], out_recv.at[kind, a], (other_f, r, b)).start()
+
+    def hand_out_keys(frame):
+        final_kv[frame, 0] = (sums[1, frame, 0] * scale).astype(jnp.bfloat16)
+        final_kv[frame, 1] = sums[1, frame, 1].astype(jnp.bfloat16)
+        for kind, ref in ((1, dk_ref), (2, dv_ref)):
+            hand_out(kind, frame, final_kv.at[frame, kind - 1], ref)
+
+    def hand_out_queries(frame, which):
+        arrived(dq_in.at[:, toks(frame)], dq_recv.at[which])
+        total = dq_sum[b, :, toks(frame)] + dq_in[:, toks(frame)].astype(jnp.float32)
+        final_q[toks(frame), :] = (total * scale).T.astype(jnp.bfloat16)
+        hand_out(0, frame, final_q.at[toks(frame)], dq_ref)
+
+    finish_keys(1 - near)
+    hand_out_keys(1 - near)
+    hand_out_queries(1 - near, 0)
+    finish_keys(near)
+    add_back(near, 1, 2)
+    hand_out_queries(near, 1)
+    for step in (-1, 1):
+        @pl.when(has_row[step])
+        def _():
+            add_back(near, 1 + step, 2)
+    hand_out_keys(near)
+
+    for kind in range(3):
+        out = (dq_ref, dk_ref, dv_ref)[kind]
+        for head in range(2):
+            arrived(out.at[:, head * feats : (head + 1) * feats], out_recv.at[kind, head])
+        arrived(final_kv.at[0, 0], out_send.at[kind])
+        for which in range(3):
+            arrived(q_source(kind, 0), q_send.at[which, kind])
+    for which in range(2):
+        arrived(kv.at[1, 0, which], kv_send.at[which])
+        arrived(dq_out.at[:, toks(0)], dq_send.at[which])
+    arrived(kv.at[1, 2], halo_send.at[1, 2])
+    arrived(grads_out.at[1, 2], ret_send.at[1, 2])
+    for step in (-1, 1):
+        @pl.when(has_row[step])
+        def _():
+            for frame in range(3):
+                arrived(kv.at[1 - step, frame], halo_send.at[1 - step, frame])
+                arrived(grads_out.at[1 + step, frame], ret_send.at[1 + step, frame])
+
+
+def local_window(rows, queries, key_vectors, value_vectors, forward_out, cotangent, log_norm):
+    shape = queries.shape
+    tokens, width = shape[3:]
+    feats = width // 2
+    flat = [x.reshape(tokens, width) for x in (queries, key_vectors, value_vectors, forward_out, cotangent)]
+    half = (tokens, feats)
+    low, full = jnp.bfloat16, jnp.float32
+    dma = pltpu.SemaphoreType.DMA
+    any_space = pl.BlockSpec(memory_space=pl.ANY)
+    outs = pl.pallas_call(
+        functools.partial(window_kernel, rows),
+        out_shape=[jax.ShapeDtypeStruct((tokens, width), low)] * 3,
+        in_specs=[any_space] * 6,
+        out_specs=[any_space] * 3,
+        scratch_shapes=[
+            pltpu.VMEM((3, 3, 2) + half, low),
+            pltpu.VMEM((2, 2, 2 * tokens, feats), low),
+            pltpu.VMEM((2, 8, 2 * tokens), full),
+            pltpu.VMEM((2, 8, tokens), full),
+            pltpu.VMEM((tokens, width), low),
+            pltpu.VMEM((tokens, width), low),
+            pltpu.VMEM((2, tokens), full),
+            pltpu.VMEM((3, 3, 2) + half, low),
+            pltpu.VMEM((3, 3, 2) + half, low),
+            pltpu.VMEM((3, 3, 2) + half, full),
+            pltpu.VMEM((2, feats, 2 * tokens), full),
+            pltpu.VMEM((feats, 2 * tokens), low),
+            pltpu.VMEM((feats, 2 * tokens), low),
+            pltpu.VMEM((2, 2) + half, low),
+            pltpu.VMEM((2 * tokens, feats), low),
+            dma((3,)), dma((2,)), dma((2, 2)), dma((3, 3)), dma((2, 2, 3)), dma((3, 3)), dma((3, 3)),
+            dma((3, 3)), dma((3, 3)), dma((2,)), dma((2,)), dma((3,)), dma((3, 2)),
+        ],
+        compiler_params=pltpu.CompilerParams(
+            collective_id=0, has_side_effects=True, vmem_limit_bytes=60 * 2**20
+        ),
+    )(*flat, log_norm.reshape(2, tokens))
+    return tuple(x.reshape(shape) for x in outs)
+
+
 def solution(mesh):
-    placed = (
-        P("frame", "row", "col", None, None),
-        P("frame", "row", "col", None, None),
-        P("frame", "row", "col", None, None),
-        P("frame", "row", "col", None, None),
-        P("frame", "row", "col", None, None),
-        P("frame", "row", "col", None, None),
-    )
+    placed = (P("frame", "row", "col", None, None),) * 6
+    sizes = dict(mesh.shape)
+    body = local
+    if sizes["frame"] == 4 and sizes["col"] == 2:
+        body = functools.partial(local_window, sizes["row"])
     return jax.shard_map(
-        local,
+        body,
         mesh=mesh,
         in_specs=placed,
-        out_specs=(
-            P("frame", "row", "col", None, None),
-            P("frame", "row", "col", None, None),
-            P("frame", "row", "col", None, None),
-        ),
+        out_specs=placed[:3],
         check_vma=False,
     )

time: 524 us -> 40.7 us (0.08); the launches traced: 517 us -> 40.5 us
  waiting for transfers between devices: 195 us -> 0 us
  local copies, waits for them, and re-layouts: 149 us -> 3.33 us
  matrix products: 88.5 us -> 0 us
  other arithmetic: 45.1 us -> 0 us
  starting transfers between devices: 37.2 us -> 0 us
  Pallas kernels: 0 us -> 36.5 us
    ppermute x12 -> x0, waiting for transfers between devices: 195 us -> none  [the longest x6 109 us: passed_along(): return lax.ppermute(x, axis, pairs)]
    dot_general x45 -> x0, matrix products: 88.5 us -> none  [the longest x9 23.3 us: slab_step(): jnp.einsum('hqk,qhd->khd', probs.astype(jnp.bfloat16), own_do, preferred_...]
    transpose x18 -> x0, local copies, waits for them, and re-layouts: 81.5 us -> none  [the longest x9 42.8 us: slab_step(): jnp.einsum('hqk,qhd->khd', probs.astype(jnp.bfloat16), own_do, preferred_...]
    ppermute x12 -> x0, starting transfers between devices: 37.2 us -> none  [the longest x6 17.4 us: passed_along(): return lax.ppermute(x, axis, pairs)]
    pallas_call x0 -> x1, Pallas kernels: none -> 36.5 us  [local_window(): pl.pallas_call(functools.partial(window_kernel, rows), out_shape=[jax.Sha...]
    reshape x47 -> x0, local copies, waits for them, and re-layouts: 27.9 us -> none  [the longest x9 8.5 us: slab_step(): grad_k.reshape(3, tile_rows, width)]
    squeeze x20 -> x0, local copies, waits for them, and re-layouts: 16.4 us -> none  [the longest x18 12.2 us: local(): grad_q, partial_sums = lax.scan(slab_step, zeros, (nearby, valid))]
    add x3 -> x0, other arithmetic: 14.7 us -> none  [the longest x1 11.3 us: reduce_frame(): lax.index_in_dim(partial_sums, 1, dim, keepdims=False) + from_next]
  transfers between devices with their start and end apart: 12 -> 0, of which waited for: 12 -> 0; matrix products, arithmetic and copies ran while one was open for 3% -> 0% of each run, Pallas kernels for 0% -> 0%
where the time goes in v2:
time: 40.7 us; the launch traced here: 40.5 us
  Pallas kernels  36.5 us (90%)
  local copies, waits for them, and re-layouts  3.33 us (8%)
  between operations  0.65 us (2%)
    pallas_call x1, Pallas kernels, local_window(): pl.pallas_call(functools.partial(window_kernel, rows), out_shape=[jax.Sha...  36.5 us
    unnamed x7, local copies, waits for them, and re-layouts  3.33 us

profile of v2, /device:TPU:17, one launch (start us, length us, event | category | flops | bytes accessed | tf_op | source)
XLA Modules:
  0.0 40.5 jit_solution(2611475944502074736)
XLA Ops:
  0.6 36.5 %shard_map.85 = (bf16[384,256]{1,0:T(8,128)(2,1)}, bf16[384,256]{1,0:T(8,128)(2,1)}, bf16[384,256]{1,0:T(8,128)(2,1)}) custom-call(bf16[384,256]{1,0:T(8,128)(2,1)} %bitcast.12, bf16[384,256]{1,0:T(8,128)(2,1)} %bitcast.13, bf16[384,256]{1,0:T(8,128)(2,1)} %bitcast.14, bf16[384,256]{1,0:T(8,128)(2,1)} %bitcast.15, bf16[384,256]{1,0:T(8,128)(2,1)} %bitcast.16, ...), custom_call_target="tpu_custom_call" | custom-call | tf_op jit(solution)/shard_map/pallas_call | solution.py:426
  37.2 0.0 copy-start.1
  37.2 1.7 %copy.12 = bf16[1,1,1,384,256]{4,3,2,1,0:T(8,128)(2,1)} copy(bf16[1,1,1,384,256]{4,3,2,1,0:T(8,128)(2,1)} %bitcast.11) | data formatting | bytes 393216
  38.8 0.0 copy-done.1
  38.8 0.0 copy-start
  38.8 0.7 %copy.13 = bf16[1,1,1,384,256]{4,3,2,1,0:T(8,128)(2,1)} copy(bf16[1,1,1,384,256]{4,3,2,1,0:T(8,128)(2,1)S(1)} %bitcast.10) | data formatting | bytes 393216
  39.5 0.3 copy-done
  39.8 0.7 %copy.14 = bf16[1,1,1,384,256]{4,3,2,1,0:T(8,128)(2,1)} copy(bf16[1,1,1,384,256]{4,3,2,1,0:T(8,128)(2,1)S(1)} %bitcast.9) | data formatting | bytes 393216
Async XLA Ops:
  37.2 1.7 %copy-start.1 = (bf16[384,256]{1,0:T(8,128)(2,1)S(1)}, bf16[384,256]{1,0:T(8,128)(2,1)}, u32[]{:S(2)}) copy-start(bf16[384,256]{1,0:T(8,128)(2,1)} %get-tuple-element.7) | copy-start | bytes 589828
  38.8 1.0 %copy-start = (bf16[384,256]{1,0:T(8,128)(2,1)S(1)}, bf16[384,256]{1,0:T(8,128)(2,1)}, u32[]{:S(2)}) copy-start(bf16[384,256]{1,0:T(8,128)(2,1)} %get-tuple-element.8) | copy-start | bytes 589828

commit v3 on v2

--- a/solution.py
+++ b/solution.py
@@ -197,42 +197,6 @@
     for kind in range(2):
         q_local(kind)
 
-    pl.semaphore_wait(
-        barrier, 4 + 2 * (has_row[-1].astype(jnp.int32) + has_row[1].astype(jnp.int32))
-    )
-
-    for kind, ref in enumerate((k_ref, v_ref)):
-        remote(
-            ref.at[:, cols(1 - a)], kv.at[1, a, kind], kv_send.at[kind], kv_recv.at[a, kind], (other_f, r, b)
-        ).start()
-    for which in range(3):
-        for kind in range(2):
-            q_remote(kind, which)
-
-    for frame in (a, 1 - a):
-        for kind in range(2):
-            arrived(kv.at[1, frame, kind], kv_recv.at[frame, kind])
-        for step in (-1, 1):
-            @pl.when(has_row[step])
-            def _():
-                remote(
-                    kv.at[1, frame], kv.at[1 - step, frame], halo_send.at[1 - step, frame],
-                    halo_recv.at[1 - step, frame], (f, r + step, b),
-                ).start()
-
-        @pl.when(near == frame)
-        def _():
-            remote(
-                kv.at[1, frame], kv.at[1, 2], halo_send.at[1, 2], halo_recv.at[1, 2], (across_f, r, b)
-            ).start()
-            for step in (-1, 1):
-                @pl.when(has_row[step])
-                def _():
-                    remote(
-                        kv.at[1, frame], kv.at[1 - step, 2], halo_send.at[1 - step, 2],
-                        halo_recv.at[1 - step, 2], (across_f, r + step, b),
-                    ).start()
-
     for load in loads:
         load.wait()
     ones = jnp.ones((8, feats), jnp.bfloat16)
@@ -247,15 +211,53 @@
         stat_own[head] = delta
         stat_own[head, 0:1, :] = log_in[head : head + 1, :] * LOG2E
     q_local(2)
+
+    pl.semaphore_wait(
+        barrier, 4 + 2 * (has_row[-1].astype(jnp.int32) + has_row[1].astype(jnp.int32))
+    )
+
+    for kind, ref in enumerate((k_ref, v_ref)):
+        remote(
+            ref.at[:, cols(1 - a)], kv.at[1, a, kind], kv_send.at[kind], kv_recv.at[a, kind], (other_f, r, b)
+        ).start()
     for which in range(3):
-        q_remote(2, which)
+        for kind in (2, 0, 1):
+            q_remote(kind, which)
+
+    for frame in (a, 1 - a):
+        for kind in range(2):
+            arrived(kv.at[1, frame, kind], kv_recv.at[frame, kind])
+        for step in (-1, 1):
+            @pl.when(has_row[step])
+            def _():
+                remote(
+                    kv.at[1, frame], kv.at[1 - step, frame], halo_send.at[1 - step, frame],
+                    halo_recv.at[1 - step, frame], (f, r + step, b),
+                ).start()
+
+        @pl.when(near == frame)
+        def _():
+            remote(
+                kv.at[1, frame], kv.at[1, 2], halo_send.at[1, 2], halo_recv.at[1, 2], (across_f, r, b)
+            ).start()
+            for step in (-1, 1):
+                @pl.when(has_row[step])
+                def _():
+                    remote(
+                        kv.at[1, frame], kv.at[1 - step, 2], halo_send.at[1 - step, 2],
+                        halo_recv.at[1 - step, 2], (across_f, r + step, b),
+                    ).start()
+
     dq_sum[...] = jnp.zeros_like(dq_sum)
+
+    def is_outer(frame):
+        return isinstance(frame, int) and frame == 2
 
     def one_block(at_row, at_frame, col, first):
         keys = kv[at_row, at_frame, 0]
         values = kv[at_row, at_frame, 1]
         keys_t = keys.T
-        if isinstance(at_frame, int) and at_frame == 2:
+        if is_outer(at_frame):
             chunks = [toks(near)]
         else:
             chunks = [pl.ds(at, 256) for at in range(0, 2 * tokens, 256)]
@@ -294,7 +296,7 @@
         remote(
             grads_out.at[at_row, at_frame], grads_in.at[2 - at_row, at_frame],
             ret_send.at[at_row, at_frame], ret_recv.at[2 - at_row, at_frame],
-            (across_f if at_frame == 2 else f, r + at_row - 1, b),
+            (across_f if is_outer(at_frame) else f, r + at_row - 1, b),
         ).start()
 
     def q_arrived(col):
@@ -338,15 +340,15 @@
     own_row(b, True)
     arrived(kv.at[1, 2], halo_recv.at[1, 2])
     one_block(1, 2, b, True)
-    both_sides(0, True, ((b, True),), False)
+    both_sides(a, True, ((b, True),), False)
     q_arrived(1 - b)
-    both_sides(0, False, ((1 - b, False),), True)
+    both_sides(a, False, ((1 - b, False),), True)
     one_block(1, 2, 1 - b, False)
     give_back(1, 2)
-    both_sides(1, True, ((b, True), (1 - b, False)), True)
+    both_sides(1 - a, True, ((b, True), (1 - b, False)), True)
+    both_sides(2, True, ((1 - b, True), (b, False)), True)
     own_row(1 - b, False)
     send_dq(1 - near, 0)
-    both_sides(2, True, ((1 - b, True), (b, False)), True)
     send_dq(near, 1)
 
     def add_back(frame, at_row, at_frame):
@@ -384,15 +386,15 @@
 
     finish_keys(1 - near)
     hand_out_keys(1 - near)
-    hand_out_queries(1 - near, 0)
     finish_keys(near)
     add_back(near, 1, 2)
-    hand_out_queries(near, 1)
     for step in (-1, 1):
         @pl.when(has_row[step])
         def _():
             add_back(near, 1 + step, 2)
     hand_out_keys(near)
+    hand_out_queries(1 - near, 0)
+    hand_out_queries(near, 1)
 
     for kind in range(3):
         out = (dq_ref, dk_ref, dv_ref)[kind]
@@ -412,6 +414,15 @@
             for frame in range(3):
                 arrived(kv.at[1 - step, frame], halo_send.at[1 - step, frame])
                 arrived(grads_out.at[1 + step, frame], ret_send.at[1 + step, frame])
+
+
+def copy_kernel(*refs):
+    sems = refs[6]
+    copies = [pltpu.make_async_copy(refs[at], refs[3 + at], sems.at[at]) for at in range(3)]
+    for copy in copies:
+        copy.start()
+    for copy in copies:
+        copy.wait()
 
 
 def local_window(rows, queries, key_vectors, value_vectors, forward_out, cotangent, log_norm):
@@ -451,6 +462,13 @@
             collective_id=0, has_side_effects=True, vmem_limit_bytes=60 * 2**20
         ),
     )(*flat, log_norm.reshape(2, tokens))
+    outs = pl.pallas_call(
+        copy_kernel,
+        out_shape=[jax.ShapeDtypeStruct((tokens, width), low)] * 3,
+        in_specs=[any_space] * 3,
+        out_specs=[any_space] * 3,
+        scratch_shapes=[dma((3,))],
+    )(*outs)
     return tuple(x.reshape(shape) for x in outs)
 
 

time: 40.7 us -> 56.3 us (1.38)
  Pallas kernels: 36.5 us -> 55.1 us
  local copies, waits for them, and re-layouts: 3.33 us -> 0 us
    pallas_call x0 -> x1, Pallas kernels: none -> 19 us  [local_window(): pl.pallas_call(copy_kernel, out_shape=[jax.ShapeDtypeStruct((tokens, widt...]
    unnamed x7 -> x0, local copies, waits for them, and re-layouts: 3.33 us -> none
where the time goes in v3:
time: 56.3 us; the launch traced here: 55.7 us
  Pallas kernels  55.1 us (98%)
  between operations  0.64 us (1%)
    pallas_call x1, Pallas kernels, local_window(): pl.pallas_call(functools.partial(window_kernel, rows), out_shape=[jax.Sha...  36.1 us
    pallas_call x1, Pallas kernels, local_window(): pl.pallas_call(copy_kernel, out_shape=[jax.ShapeDtypeStruct((tokens, widt...  19 us

profile of v3, /device:TPU:17, one launch (start us, length us, event | category | flops | bytes accessed | tf_op | source)
XLA Modules:
  0.0 55.7 jit_solution(15897530631738432294)
XLA Ops:
  0.6 36.1 %shard_map.85 = (bf16[384,256]{1,0:T(8,128)(2,1)}, bf16[384,256]{1,0:T(8,128)(2,1)}, bf16[384,256]{1,0:T(8,128)(2,1)}) custom-call(bf16[384,256]{1,0:T(8,128)(2,1)} %bitcast.9, bf16[384,256]{1,0:T(8,128)(2,1)} %bitcast.10, bf16[384,256]{1,0:T(8,128)(2,1)} %bitcast.11, bf16[384,256]{1,0:T(8,128)(2,1)} %bitcast.12, bf16[384,256]{1,0:T(8,128)(2,1)} %bitcast.13, ...), custom_call_target="tpu_custom_call" | custom-call | tf_op jit(solution)/shard_map/pallas_call | solution.py:437
  36.8 19.0 %shard_map.86 = (bf16[384,256]{1,0:T(8,128)(2,1)}, bf16[384,256]{1,0:T(8,128)(2,1)}, bf16[384,256]{1,0:T(8,128)(2,1)}) custom-call(bf16[384,256]{1,0:T(8,128)(2,1)} %get-tuple-element.9.refs_0_, bf16[384,256]{1,0:T(8,128)(2,1)} %get-tuple-element.10.refs_1_, bf16[384,256]{1,0:T(8,128)(2,1)} %get-tuple-element.11.refs_2_), custom_call_target="tpu_custom_call" | custom-call | tf_op jit(solution)/shard_map/pallas_call | solution.py:465

commit v4 on v3

--- a/solution.py
+++ b/solution.py
@@ -262,28 +262,22 @@
         else:
             chunks = [pl.ds(at, 256) for at in range(0, 2 * tokens, 256)]
 
-        def products(some):
-            q_part = qd[col, 0, some, :]
-            do_part = qd[col, 1, some, :]
-            scores = lax.dot_general(keys, q_part, along, preferred_element_type=jnp.float32)
-            dprobs = lax.dot_general(values, do_part, along, preferred_element_type=jnp.float32)
-            return q_part, do_part, scores, dprobs
-
-        dk = dv = None
-        upcoming = products(chunks[0])
-        for at, some in enumerate(chunks):
-            q_part, do_part, scores, dprobs = upcoming
-            if at + 1 < len(chunks):
-                upcoming = products(chunks[at + 1])
+        all_probs, all_dscores = [], []
+        for some in chunks:
+            scores = lax.dot_general(keys, qd[col, 0, some, :], along, preferred_element_type=jnp.float32)
+            dprobs = lax.dot_general(values, qd[col, 1, some, :], along, preferred_element_type=jnp.float32)
             probs = jnp.exp2(scores * (scale * LOG2E) - stat[col, 0:1, some])
-            dscores = probs * (dprobs - stat[col, 1:2, some])
-            probs = probs.astype(jnp.bfloat16)
-            dscores = dscores.astype(jnp.bfloat16)
-            dv_part = jnp.dot(probs, do_part, preferred_element_type=jnp.float32)
-            dk_part = jnp.dot(dscores, q_part, preferred_element_type=jnp.float32)
-            dv = dv_part if dv is None else dv + dv_part
-            dk = dk_part if dk is None else dk + dk_part
+            dscores = (probs * (dprobs - stat[col, 1:2, some])).astype(jnp.bfloat16)
             dq_sum[col, :, some] += jnp.dot(keys_t, dscores, preferred_element_type=jnp.float32)
+            all_probs.append(probs.astype(jnp.bfloat16))
+            all_dscores.append(dscores)
+        together = chunks[0] if len(chunks) == 1 else pl.ds(0, 2 * tokens)
+        dv = jnp.dot(
+            jnp.concatenate(all_probs, axis=1), qd[col, 1, together, :], preferred_element_type=jnp.float32
+        )
+        dk = jnp.dot(
+            jnp.concatenate(all_dscores, axis=1), qd[col, 0, together, :], preferred_element_type=jnp.float32
+        )
         if first:
             sums[at_row, at_frame, 0] = dk
             sums[at_row, at_frame, 1] = dv
@@ -434,6 +428,7 @@
     low, full = jnp.bfloat16, jnp.float32
     dma = pltpu.SemaphoreType.DMA
     any_space = pl.BlockSpec(memory_space=pl.ANY)
+    vmem = pl.BlockSpec(memory_space=pltpu.VMEM)
     outs = pl.pallas_call(
         functools.partial(window_kernel, rows),
         out_shape=[jax.ShapeDtypeStruct((tokens, width), low)] * 3,
@@ -465,7 +460,7 @@
     outs = pl.pallas_call(
         copy_kernel,
         out_shape=[jax.ShapeDtypeStruct((tokens, width), low)] * 3,
-        in_specs=[any_space] * 3,
+        in_specs=[vmem] * 3,
         out_specs=[any_space] * 3,
         scratch_shapes=[dma((3,))],
     )(*outs)

time: 56.3 us -> 39.2 us (0.70)
  Pallas kernels: 55.1 us -> 38.4 us
    pallas_call x1, Pallas kernels: 19 us -> 1.95 us  [local_window(): pl.pallas_call(copy_kernel, out_shape=[jax.ShapeDtypeStruct((tokens, widt...]
where the time goes in v4:
time: 39.2 us; the launch traced here: 39.1 us
  Pallas kernels  38.4 us (98%)
  between operations  0.64 us (2%)
    pallas_call x1, Pallas kernels, local_window(): pl.pallas_call(functools.partial(window_kernel, rows), out_shape=[jax.Sha...  36.5 us
    pallas_call x1, Pallas kernels, local_window(): pl.pallas_call(copy_kernel, out_shape=[jax.ShapeDtypeStruct((tokens, widt...  1.95 us

profile of v4, /device:TPU:17, one launch (start us, length us, event | category | flops | bytes accessed | tf_op | source)
XLA Modules:
  0.0 39.1 jit_solution(2980929842655272356)
XLA Ops:
  0.6 36.5 %shard_map.85 = (bf16[384,256]{1,0:T(8,128)(2,1)}, bf16[384,256]{1,0:T(8,128)(2,1)}, bf16[384,256]{1,0:T(8,128)(2,1)}) custom-call(bf16[384,256]{1,0:T(8,128)(2,1)} %bitcast.9, bf16[384,256]{1,0:T(8,128)(2,1)} %bitcast.10, bf16[384,256]{1,0:T(8,128)(2,1)} %bitcast.11, bf16[384,256]{1,0:T(8,128)(2,1)} %bitcast.12, bf16[384,256]{1,0:T(8,128)(2,1)} %bitcast.13, ...), custom_call_target="tpu_custom_call" | custom-call | tf_op jit(solution)/shard_map/pallas_call | solution.py:432
  37.1 1.9 %shard_map.86 = (bf16[384,256]{1,0:T(8,128)(2,1)}, bf16[384,256]{1,0:T(8,128)(2,1)}, bf16[384,256]{1,0:T(8,128)(2,1)}) custom-call(bf16[384,256]{1,0:T(8,128)(2,1)} %get-tuple-element.9.refs_0_, bf16[384,256]{1,0:T(8,128)(2,1)} %get-tuple-element.10.refs_1_, bf16[384,256]{1,0:T(8,128)(2,1)} %get-tuple-element.11.refs_2_), custom_call_target="tpu_custom_call" | custom-call | tf_op jit(solution)/shard_map/pallas_call | solution.py:460

commit v5 on v4

--- a/solution.py
+++ b/solution.py
@@ -127,9 +127,9 @@
     rows,
     q_ref, k_ref, v_ref, o_ref, do_ref, log_ref,
     dq_ref, dk_ref, dv_ref,
-    kv, qd, stat, stat_own, o_in, do_in, log_in, grads_out, grads_in, sums, dq_sum, dq_out, dq_in,
+    kv, qd, turned, stat, stat_own, o_in, do_in, log_in, grads_out, grads_in, sums, dq_sum, dq_out, dq_in,
     final_kv, final_q,
-    load_sem, kv_send, kv_recv, q_send, q_recv, halo_send, halo_recv,
+    load_sem, kv_send, kv_recv, q_send, q_recv, halo_send, halo_recv, corner_send, corner_recv,
     ret_send, ret_recv, dq_send, dq_recv, out_send, out_recv,
 ):
     f, r, b = lax.axis_index("frame"), lax.axis_index("row"), lax.axis_index("col")
@@ -224,9 +224,13 @@
         for kind in (2, 0, 1):
             q_remote(kind, which)
 
-    for frame in (a, 1 - a):
+    for frame in (near, 1 - near):
         for kind in range(2):
             arrived(kv.at[1, frame, kind], kv_recv.at[frame, kind])
+        if frame is near:
+            remote(
+                kv.at[1, frame], kv.at[1, 2], halo_send.at[1, 2], halo_recv.at[1, 2], (across_f, r, b)
+            ).start()
         for step in (-1, 1):
             @pl.when(has_row[step])
             def _():
@@ -235,23 +239,30 @@
                     halo_recv.at[1 - step, frame], (f, r + step, b),
                 ).start()
 
-        @pl.when(near == frame)
-        def _():
-            remote(
-                kv.at[1, frame], kv.at[1, 2], halo_send.at[1, 2], halo_recv.at[1, 2], (across_f, r, b)
-            ).start()
-            for step in (-1, 1):
-                @pl.when(has_row[step])
-                def _():
-                    remote(
-                        kv.at[1, frame], kv.at[1 - step, 2], halo_send.at[1 - step, 2],
-                        halo_recv.at[1 - step, 2], (across_f, r + step, b),
-                    ).start()
-
     dq_sum[...] = jnp.zeros_like(dq_sum)
 
     def is_outer(frame):
         return isinstance(frame, int) and frame == 2
+
+    by_row, by_frame = pl.ds(0, tokens // 3), pl.ds(tokens // 3, tokens - tokens // 3)
+
+    def pass_corners():
+        arrived(kv.at[1, 2], halo_recv.at[1, 2])
+        for step in (-1, 1):
+            @pl.when(has_row[step])
+            def _():
+                remote(
+                    kv.at[1, 2, :, by_row], kv.at[1 - step, 2, :, by_row], halo_send.at[1 - step, 2],
+                    corner_recv.at[1 - step, 0], (f, r + step, b),
+                ).start()
+        for step in (-1, 1):
+            @pl.when(has_row[step])
+            def _():
+                arrived(kv.at[1 + step, near], halo_recv.at[1 + step, near])
+                remote(
+                    kv.at[1 + step, near, :, by_frame], kv.at[1 + step, 2, :, by_frame],
+                    corner_send.at[1 + step], corner_recv.at[1 + step, 1], (across_f, r, b),
+                ).start()
 
     def one_block(at_row, at_frame, col, first):
         keys = kv[at_row, at_frame, 0]
@@ -264,8 +275,8 @@
 
         all_probs, all_dscores = [], []
         for some in chunks:
-            scores = lax.dot_general(keys, qd[col, 0, some, :], along, preferred_element_type=jnp.float32)
-            dprobs = lax.dot_general(values, qd[col, 1, some, :], along, preferred_element_type=jnp.float32)
+            scores = jnp.dot(keys, turned[col, 0, :, some], preferred_element_type=jnp.float32)
+            dprobs = jnp.dot(values, turned[col, 1, :, some], preferred_element_type=jnp.float32)
             probs = jnp.exp2(scores * (scale * LOG2E) - stat[col, 0:1, some])
             dscores = (probs * (dprobs - stat[col, 1:2, some])).astype(jnp.bfloat16)
             dq_sum[col, :, some] += jnp.dot(keys_t, dscores, preferred_element_type=jnp.float32)
@@ -297,6 +308,8 @@
         for frame in range(2):
             for kind in range(3):
                 arrived(q_slot(kind, frame, col), q_recv.at[col, frame, kind])
+        for kind in range(2):
+            turned[col, kind] = qd[col, kind].T
 
     def own_row(col, first):
         def body(frame, carry):
@@ -312,7 +325,10 @@
 
             @pl.when((to_row >= 0) & (to_row < rows))
             def _():
-                if wait:
+                if wait and is_outer(frame):
+                    arrived(kv.at[at_row, 2, :, by_row], corner_recv.at[at_row, 0])
+                    arrived(kv.at[at_row, 2, :, by_frame], corner_recv.at[at_row, 1])
+                elif wait:
                     arrived(kv.at[at_row, frame], halo_recv.at[at_row, frame])
                 for col, first in blocks:
                     one_block(at_row, frame, col, first)
@@ -330,20 +346,22 @@
             (f, r, 1 - b),
         ).start()
 
+    far = 1 - near
     q_arrived(b)
     own_row(b, True)
-    arrived(kv.at[1, 2], halo_recv.at[1, 2])
+    pass_corners()
     one_block(1, 2, b, True)
-    both_sides(a, True, ((b, True),), False)
+    both_sides(near, False, ((b, True),), False)
     q_arrived(1 - b)
-    both_sides(a, False, ((1 - b, False),), True)
     one_block(1, 2, 1 - b, False)
     give_back(1, 2)
-    both_sides(1 - a, True, ((b, True), (1 - b, False)), True)
+    both_sides(near, False, ((1 - b, False),), True)
     both_sides(2, True, ((1 - b, True), (b, False)), True)
     own_row(1 - b, False)
-    send_dq(1 - near, 0)
+    both_sides(far, True, ((1 - b, True),), False)
+    send_dq(far, 0)
     send_dq(near, 1)
+    both_sides(far, False, ((b, False),), True)
 
     def add_back(frame, at_row, at_frame):
         arrived(grads_in.at[at_row, at_frame], ret_recv.at[at_row, at_frame])
@@ -378,8 +396,6 @@
         final_q[toks(frame), :] = (total * scale).T.astype(jnp.bfloat16)
         hand_out(0, frame, final_q.at[toks(frame)], dq_ref)
 
-    finish_keys(1 - near)
-    hand_out_keys(1 - near)
     finish_keys(near)
     add_back(near, 1, 2)
     for step in (-1, 1):
@@ -387,8 +403,10 @@
         def _():
             add_back(near, 1 + step, 2)
     hand_out_keys(near)
-    hand_out_queries(1 - near, 0)
     hand_out_queries(near, 1)
+    hand_out_queries(far, 0)
+    finish_keys(far)
+    hand_out_keys(far)
 
     for kind in range(3):
         out = (dq_ref, dk_ref, dv_ref)[kind]
@@ -405,8 +423,11 @@
     for step in (-1, 1):
         @pl.when(has_row[step])
         def _():
+            arrived(kv.at[1, 2, :, by_row], halo_send.at[1 - step, 2])
+            arrived(kv.at[1, 2, :, by_frame], corner_send.at[1 + step])
+            for frame in range(2):
+                arrived(kv.at[1 - step, frame], halo_send.at[1 - step, frame])
             for frame in range(3):
-                arrived(kv.at[1 - step, frame], halo_send.at[1 - step, frame])
                 arrived(grads_out.at[1 + step, frame], ret_send.at[1 + step, frame])
 
 
@@ -437,6 +458,7 @@
         scratch_shapes=[
             pltpu.VMEM((3, 3, 2) + half, low),
             pltpu.VMEM((2, 2, 2 * tokens, feats), low),
+            pltpu.VMEM((2, 2, feats, 2 * tokens), low),
             pltpu.VMEM((2, 8, 2 * tokens), full),
             pltpu.VMEM((2, 8, tokens), full),
             pltpu.VMEM((tokens, width), low),
@@ -450,7 +472,7 @@
             pltpu.VMEM((feats, 2 * tokens), low),
             pltpu.VMEM((2, 2) + half, low),
             pltpu.VMEM((2 * tokens, feats), low),
-            dma((3,)), dma((2,)), dma((2, 2)), dma((3, 3)), dma((2, 2, 3)), dma((3, 3)), dma((3, 3)),
+            dma((3,)), dma((2,)), dma((2, 2)), dma((3, 3)), dma((2, 2, 3)), dma((3, 3)), dma((3, 3)), dma((3,)), dma((3, 2)),
             dma((3, 3)), dma((3, 3)), dma((2,)), dma((2,)), dma((3,)), dma((3, 2)),
         ],
         compiler_params=pltpu.CompilerParams(

time: 39.2 us -> 38.3 us (0.977); the launches traced: 39.1 us -> 37.5 us
  Pallas kernels: 38.4 us -> 36.9 us
    pallas_call x1, Pallas kernels: 36.5 us -> 35 us  [local_window(): pl.pallas_call(functools.partial(window_kernel, rows), out_shape=[jax.Sha...]
where the time goes in v5:
time: 38.3 us; the launch traced here: 37.5 us
  Pallas kernels  36.9 us (96%)
  between operations  0.64 us (2%)
    pallas_call x1, Pallas kernels, local_window(): pl.pallas_call(functools.partial(window_kernel, rows), out_shape=[jax.Sha...  35 us
    pallas_call x1, Pallas kernels, local_window(): pl.pallas_call(copy_kernel, out_shape=[jax.ShapeDtypeStruct((tokens, widt...  1.95 us

profile of v5, /device:TPU:17, one launch (start us, length us, event | category | flops | bytes accessed | tf_op | source)
XLA Modules:
  0.0 37.5 jit_solution(11572014162988833176)
XLA Ops:
  0.6 35.0 %shard_map.85 = (bf16[384,256]{1,0:T(8,128)(2,1)}, bf16[384,256]{1,0:T(8,128)(2,1)}, bf16[384,256]{1,0:T(8,128)(2,1)}) custom-call(bf16[384,256]{1,0:T(8,128)(2,1)} %bitcast.9, bf16[384,256]{1,0:T(8,128)(2,1)} %bitcast.10, bf16[384,256]{1,0:T(8,128)(2,1)} %bitcast.11, bf16[384,256]{1,0:T(8,128)(2,1)} %bitcast.12, bf16[384,256]{1,0:T(8,128)(2,1)} %bitcast.13, ...), custom_call_target="tpu_custom_call" | custom-call | tf_op jit(solution)/shard_map/pallas_call | solution.py:453
  35.6 1.9 %shard_map.86 = (bf16[384,256]{1,0:T(8,128)(2,1)}, bf16[384,256]{1,0:T(8,128)(2,1)}, bf16[384,256]{1,0:T(8,128)(2,1)}) custom-call(bf16[384,256]{1,0:T(8,128)(2,1)} %get-tuple-element.9.refs_0_, bf16[384,256]{1,0:T(8,128)(2,1)} %get-tuple-element.10.refs_1_, bf16[384,256]{1,0:T(8,128)(2,1)} %get-tuple-element.11.refs_2_), custom_call_target="tpu_custom_call" | custom-call | tf_op jit(solution)/shard_map/pallas_call | solution.py:482

commit v6 on v5

--- a/solution.py
+++ b/solution.py
@@ -432,12 +432,16 @@
 
 
 def copy_kernel(*refs):
-    sems = refs[6]
-    copies = [pltpu.make_async_copy(refs[at], refs[3 + at], sems.at[at]) for at in range(3)]
-    for copy in copies:
-        copy.start()
-    for copy in copies:
-        copy.wait()
+    held, sems = refs[6], refs[7]
+    loads = [pltpu.make_async_copy(refs[at], held.at[at], sems.at[at]) for at in range(3)]
+    stores = [pltpu.make_async_copy(held.at[at], refs[3 + at], sems.at[3 + at]) for at in range(3)]
+    for load in loads:
+        load.start()
+    for load, store in zip(loads, stores):
+        load.wait()
+        store.start()
+    for store in stores:
+        store.wait()
 
 
 def local_window(rows, queries, key_vectors, value_vectors, forward_out, cotangent, log_norm):
@@ -449,7 +453,6 @@
     low, full = jnp.bfloat16, jnp.float32
     dma = pltpu.SemaphoreType.DMA
     any_space = pl.BlockSpec(memory_space=pl.ANY)
-    vmem = pl.BlockSpec(memory_space=pltpu.VMEM)
     outs = pl.pallas_call(
         functools.partial(window_kernel, rows),
         out_shape=[jax.ShapeDtypeStruct((tokens, width), low)] * 3,
@@ -482,9 +485,9 @@
     outs = pl.pallas_call(
         copy_kernel,
         out_shape=[jax.ShapeDtypeStruct((tokens, width), low)] * 3,
-        in_specs=[vmem] * 3,
+        in_specs=[any_space] * 3,
         out_specs=[any_space] * 3,
-        scratch_shapes=[dma((3,))],
+        scratch_shapes=[pltpu.VMEM((3, tokens, width), low), dma((6,))],
     )(*outs)
     return tuple(x.reshape(shape) for x in outs)
 

time: 38.3 us -> 38.2 us (level)
  no operation moved by 1% of the time
where the time goes in v6:
time: 38.2 us; the launch traced here: 37.4 us
  Pallas kernels  36.8 us (96%)
  between operations  0.64 us (2%)
    pallas_call x1, Pallas kernels, local_window(): pl.pallas_call(functools.partial(window_kernel, rows), out_shape=[jax.Sha...  35 us
    pallas_call x1, Pallas kernels, local_window(): pl.pallas_call(copy_kernel, out_shape=[jax.ShapeDtypeStruct((tokens, widt...  1.84 us

profile of v6, /device:TPU:17, one launch (start us, length us, event | category | flops | bytes accessed | tf_op | source)
XLA Modules:
  0.0 37.4 jit_solution(13525876632043529489)
XLA Ops:
  0.6 35.0 %shard_map.85 = (bf16[384,256]{1,0:T(8,128)(2,1)}, bf16[384,256]{1,0:T(8,128)(2,1)}, bf16[384,256]{1,0:T(8,128)(2,1)}) custom-call(bf16[384,256]{1,0:T(8,128)(2,1)} %bitcast.9, bf16[384,256]{1,0:T(8,128)(2,1)} %bitcast.10, bf16[384,256]{1,0:T(8,128)(2,1)} %bitcast.11, bf16[384,256]{1,0:T(8,128)(2,1)} %bitcast.12, bf16[384,256]{1,0:T(8,128)(2,1)} %bitcast.13, ...), custom_call_target="tpu_custom_call" | custom-call | tf_op jit(solution)/shard_map/pallas_call | solution.py:456
  35.6 1.8 %shard_map.86 = (bf16[384,256]{1,0:T(8,128)(2,1)}, bf16[384,256]{1,0:T(8,128)(2,1)}, bf16[384,256]{1,0:T(8,128)(2,1)}) custom-call(bf16[384,256]{1,0:T(8,128)(2,1)} %get-tuple-element.9.refs_0_, bf16[384,256]{1,0:T(8,128)(2,1)} %get-tuple-element.10.refs_1_, bf16[384,256]{1,0:T(8,128)(2,1)} %get-tuple-element.11.refs_2_), custom_call_target="tpu_custom_call" | custom-call | tf_op jit(solution)/shard_map/pallas_call | solution.py:485
